TPU v7x, 32 devices: a whole 2x2x4 slice. The times are simulated.
32 devices in a mesh: row: 8 (over z, y), col: 4 (over x, core).
Axes of the slice: x: 2, y: 2, z: 4, core: 2. Of those that a mesh axis runs over, the one named last changes fastest.
Arguments:
- panel: float32 [8, 8, 256, 256], P(None, 'row', None, 'col'), may hold values from -0.1875 to 0.1875
- slab: bfloat16 [8, 8, 256, 4, 4, 256], P(None, 'row', None, None, 'col'), may hold values from -6 to 6
- cotangent: bfloat16 [8, 8, 256, 4, 4, 256], P(None, 'row', None, None, 'col'), may hold values from -0.0625 to 0.0625
- inverse: float32 [256, 256], replicated, may hold values from -2 to 8, as said below
Outputs:
- updated: bfloat16 [8, 8, 256, 4, 4, 256], P(None, 'row', None, None, 'col')
- grad_panel: float32 [8, 8, 256, 256], P(None, 'row', None, 'col')
- grad_inverse: float32 [256, 256], P(None, 'col')
Inputs may be any that keep to these rules, and one draw needn't show every extreme that they name: `inverse`: lower triangular; diagonal entries between 4 and 8.
All inputs are finite; a program needn't handle non-finite values.
Results may differ from a plain program's by a relative error of at most 0.015.
Values may be sent and summed in bfloat16 or wider, within the bound.
No kernel may reach another device: no remote copies, remote signals or barrier semaphores. Data moves between devices by JAX's collectives and lax.ppermute only.
A program may use at most 128 MiB of HBM per device.

v0:
```python
import functools

import jax
import jax.numpy as jnp
from jax import lax
from jax.experimental import pallas as pl
from jax.experimental.pallas import tpu as pltpu
from jax.sharding import PartitionSpec as P

BOTH = ("row", "col")
F32 = jnp.float32
BF16 = jnp.bfloat16
LANES = 128
VMEM = pl.BlockSpec(memory_space=pltpu.VMEM)
SMEM = pl.BlockSpec(memory_space=pltpu.SMEM)
STREAMED = 58
ANY = pl.BlockSpec(memory_space=pl.ANY)


def bits_of(count):
    return [1 << b for b in reversed(range(count.bit_length() - 1))]


def reversed_bits(value, count):
    width = count.bit_length() - 1
    place = 0
    for b in range(width):
        place = place + (((value >> b) & 1) << (width - 1 - b))
    return place


def dot(a, b, dims, precision=None):
    return lax.dot_general(a, b, (dims, ((), ())), precision=precision, preferred_element_type=F32)


def whole(shape):
    return pl.BlockSpec(shape, lambda *_: (0,) * len(shape))


def params(mib=24):
    return pltpu.CompilerParams(vmem_limit_bytes=mib * 2**20)


def cost(flops, nbytes):
    return pl.CostEstimate(flops=flops, bytes_accessed=nbytes, transcendentals=0)


def unmix_kernel(slabs, tile, x_ref, o_ref, token_ref, wide_ref, ins, outs, in_sems, out_sems):
    step, steps = pl.program_id(0), ins.shape[0]
    size = ins.shape[1]

    def copy_in(t):
        at = pl.multiple_of(t * size, size)
        return pltpu.make_async_copy(x_ref.at[pl.ds(at, size)], ins.at[t], in_sems.at[t])

    def copy_out(t):
        at = pl.multiple_of(t * tile, tile)
        return pltpu.make_async_copy(outs.at[t], o_ref.at[pl.ds(at, tile)], out_sems.at[t])

    @pl.when(step == 0)
    def _():
        for t in range(steps):
            copy_in(t).start()
        token_ref[...] = jnp.zeros_like(token_ref)

    copy_in(step).wait()
    halves = tile // LANES
    wide_ref[...] = ins[step].astype(F32)
    for s in range(slabs):
        for h in range(halves):
            part = wide_ref[pl.ds(h * slabs + s, tile, stride=halves * slabs), :]
            outs[step, :, s * tile + h * LANES : s * tile + (h + 1) * LANES] = part.astype(BF16)
    copy_out(step).start()

    @pl.when(step == steps - 1)
    def _():
        for t in range(steps):
            copy_out(t).wait()


def q_kernel(n_row, n_col, groups, place_ref, *refs):
    parts, (inv_ref, g_ref, q_ref, e_ref, pt_ref, m_ref, ins, sems) = refs[:n_col], refs[n_col:]
    tiles, strip, tile = parts[0].shape
    s = pl.program_id(0)
    row, col = place_ref[0], place_ref[1]
    group, rho = row // n_col, (row % n_col) ^ (n_col // 2)

    def copy_in(at):
        columns = pl.ds(pl.multiple_of(at * tile, tile), tile)
        return pltpu.make_async_copy(g_ref.at[:, columns], ins.at[at], sems.at[at])

    @pl.when(s == 0)
    def _():
        for at in range(ins.shape[0]):
            copy_in(at).start()
        mat = dot(inv_ref[...], inv_ref[...], ((0,), (0,)), lax.Precision.HIGHEST)
        high = mat.astype(BF16)
        m_ref[0] = high
        m_ref[1] = (mat - high.astype(F32)).astype(BF16)
        for q in range(n_col):
            at = pl.multiple_of((col ^ q) * strip, strip)
            for t in range(tiles):
                pt_ref[pl.ds(at, strip), t * tile : (t + 1) * tile] = parts[q][t]

    copy_in(s).wait()
    q_ref[s] = dot(pt_ref[...], ins[s], ((1,), (0,))).astype(BF16)

    @pl.when(s == pl.num_programs(0) - 1)
    def _():
        for at in range(q_ref.shape[0]):
            q_val = q_ref[at]
            e_val = -(dot(m_ref[0], q_val, ((1,), (0,))) + dot(m_ref[1], q_val, ((1,), (0,))))
            e_val = e_val.astype(BF16)
            slot, other = at // groups, group ^ (at % groups)
            for r in range(n_col):
                e_ref[reversed_bits(rho ^ r, n_col), other, slot] = e_val[r * strip : (r + 1) * strip]


def w_kernel(n_row, n_col, groups, place_ref, *refs):
    tops, (m_ref, inv_ref, q_ref, _, w_ref, wt_ref, gi_ref, top_all) = refs[:n_col], refs[n_col:]
    slots, strip, tile = tops[0].shape[1:]
    slabs = slots * groups
    row, col = place_ref[0], place_ref[1]
    group, rho = row // n_col, (row % n_col) ^ (n_col // 2)
    for p in range(n_row):
        at = pl.multiple_of((rho ^ (p % n_col)) * strip, strip)
        for slot in range(slots):
            s = slot * groups + (group ^ (p // n_col))
            top_all[s, pl.ds(at, strip), :] = tops[p % n_col][p // n_col, slot]
    z = jnp.zeros((tile, tile), F32)
    for s in range(slabs):
        top = top_all[s]
        w = dot(m_ref[0], top, ((1,), (0,))) + dot(m_ref[1], top, ((1,), (0,)))
        w = w.astype(BF16)
        w_ref[:, s * tile : (s + 1) * tile] = w
        wt_ref[s * tile : (s + 1) * tile, :] = w.T
        z = z + dot(top, q_ref[s], ((1,), (1,)))
    z = z + z.T
    gi = -dot(z, inv_ref[...], ((1,), (1,)), lax.Precision.HIGHEST)
    for r in range(n_col):
        gi_ref[col ^ r] = gi[r * strip : (r + 1) * strip].astype(BF16)


def h_kernel(n_col, place_ref, wt_ref, g_ref, h_ref):
    strip = h_ref.shape[2]
    t = pl.program_id(0)
    col = place_ref[1]
    tile = h_ref.shape[3]
    pair = -dot(g_ref[...], wt_ref[...], ((1,), (0,)))
    pair = pair.astype(BF16)
    for k in range(2):
        h = pair[k * tile : (k + 1) * tile].T
        for r in range(n_col):
            h_ref[reversed_bits(col ^ r, n_col), 2 * t + k] = h[r * strip : (r + 1) * strip]


def update_kernel(slabs, tile, pt_ref, w_ref, x_ref, *refs):
    o_ref, wide_ref = refs[-2:]
    halves = tile // LANES
    for k in range(2):
        product = dot(pt_ref[:, k * tile : (k + 1) * tile], w_ref[...], ((0,), (0,)))
        for s in range(slabs):
            for h in range(halves):
                part = product[:, s * tile + h * LANES : s * tile + (h + 1) * LANES]
                at = (k * tile * halves + h) * slabs + s
                wide_ref[pl.ds(at, tile, stride=halves * slabs), :] = part
    o_ref[...] = (x_ref[...].astype(F32) - wide_ref[...]).astype(BF16)


def mixed_rows(x):
    tiles, _, tile, slabs, _, _ = x.shape
    x = x.reshape(tiles, tile, slabs, tile // LANES, LANES).transpose(0, 1, 3, 2, 4)
    return x.reshape(-1, LANES)


def per_device(panel, slab, cotangent, inverse):
    tiles, _, tile, strip = panel.shape
    slabs = slab.shape[3]
    n_row = lax.axis_size("row")
    n_col = lax.axis_size("col")
    groups = n_row // n_col
    slots = slabs // groups
    width = slabs * tile
    rows = tiles * tile
    mixed = tile * width // LANES
    place = jnp.stack([lax.axis_index("row"), lax.axis_index("col")]).astype(jnp.int32)

    def permute_row(value, bit):
        return lax.ppermute(value, "row", [(i, i ^ bit) for i in range(n_row)])

    def permute_col(value, bit):
        return lax.ppermute(value, "col", [(i, i ^ bit) for i in range(n_col)])

    far = n_col // 2

    def transpose(value, across, back=False):
        pairs = []
        for m in range(groups):
            for a in range(n_col):
                for b in range(n_col):
                    here = (m * n_col + a) * n_col + b
                    there = ((m ^ across) * n_col + (b ^ far)) * n_col + a
                    pairs.append((there, here) if back else (here, there))
        return lax.ppermute(value, BOTH, pairs)

    own = panel.reshape(tiles, tile, strip).transpose(0, 2, 1).astype(BF16)
    high, *lower = bits_of(n_col)
    half = tiles // 2
    parts = {0: own, high: permute_col(own, high)}
    if lower:
        parts[1] = permute_col(own, 1)
    tops = [transpose(own[:slots], m) for m in range(groups)]
    cot, token = pl.pallas_call(
        functools.partial(unmix_kernel, slabs, tile),
        grid=(tiles,),
        in_specs=[ANY],
        out_specs=[ANY, whole((8, LANES))],
        out_shape=[
            jax.ShapeDtypeStruct((rows, width), BF16),
            jax.ShapeDtypeStruct((8, LANES), F32),
        ],
        scratch_shapes=[
            pltpu.VMEM((mixed, LANES), F32),
            pltpu.VMEM((tiles, mixed, LANES), BF16),
            pltpu.VMEM((tiles, tile, width), BF16),
            pltpu.SemaphoreType.DMA((tiles,)),
            pltpu.SemaphoreType.DMA((tiles,)),
        ],
        compiler_params=params(STREAMED),
        cost_estimate=cost(0, 4 * rows * width),
    )(mixed_rows(cotangent))

    tops, parts, token = lax.optimization_barrier((tops, parts, token))

    top = jnp.stack(tops)
    tops = [top] + [permute_row(top, q) for q in range(1, n_col)]
    for bit in lower:
        for q in range(0, n_col, 2 * bit):
            if q | bit not in parts:
                parts[q | bit] = permute_col(parts[q], bit)

    q_sum, e_part, panel_all, mat = pl.pallas_call(
        functools.partial(q_kernel, n_row, n_col, groups),
        grid=(slabs,),
        in_specs=[SMEM]
        + [whole((tiles, strip, tile))] * n_col
        + [whole((tile, tile)), ANY],
        out_specs=[
            whole((slabs, tile, tile)),
            whole((n_col, groups, slots, strip, tile)),
            whole((tile, rows)),
            whole((2, tile, tile)),
        ],
        out_shape=[
            jax.ShapeDtypeStruct((slabs, tile, tile), BF16),
            jax.ShapeDtypeStruct((n_col, groups, slots, strip, tile), BF16),
            jax.ShapeDtypeStruct((tile, rows), BF16),
            jax.ShapeDtypeStruct((2, tile, tile), BF16),
        ],
        scratch_shapes=[
            pltpu.VMEM((slabs, rows, tile), BF16),
            pltpu.SemaphoreType.DMA((slabs,)),
        ],
        compiler_params=params(STREAMED - 10),
        cost_estimate=cost(2 * rows * width * tile, 2 * rows * (width + tile)),
    )(place, *[parts[q] for q in range(n_col)], inverse, cot)

    w, w_flip, gi = pl.pallas_call(
        functools.partial(w_kernel, n_row, n_col, groups),
        in_specs=[SMEM] + [VMEM] * (n_col + 3) + [ANY],
        out_specs=[VMEM, VMEM, VMEM],
        out_shape=[
            jax.ShapeDtypeStruct((tile, width), BF16),
            jax.ShapeDtypeStruct((width, tile), BF16),
            jax.ShapeDtypeStruct((n_col, strip, tile), BF16),
        ],
        scratch_shapes=[pltpu.VMEM((slabs, tile, tile), BF16)],
        compiler_params=params(),
        cost_estimate=cost(tile, tile),
    )(place, *tops, mat, inverse, q_sum, token)

    def h_part(first, count):
        return pl.pallas_call(
            functools.partial(h_kernel, n_col),
            grid=(count // 2,),
            in_specs=[
                SMEM,
                whole((width, tile)),
                pl.BlockSpec((2 * tile, width), lambda t: (t + first // 2, 0)),
            ],
            out_specs=whole((n_col, count, strip, tile)),
            out_shape=jax.ShapeDtypeStruct((n_col, count, strip, tile), BF16),
            compiler_params=params(),
            cost_estimate=cost(tile, tile),
        )(place, w_flip, cot)

    def update(first, count, previous):
        return pl.pallas_call(
            functools.partial(update_kernel, slabs, tile),
            grid=(count // 2,),
            in_specs=[
                pl.BlockSpec((tile, 2 * tile), lambda t: (0, t + first // 2)),
                whole((tile, width)),
                pl.BlockSpec((2 * mixed, LANES), lambda t: (t + first // 2, 0)),
            ]
            + [ANY] * len(previous),
            out_specs=pl.BlockSpec((2 * mixed, LANES), lambda t: (t + first // 2, 0)),
            out_shape=jax.ShapeDtypeStruct((tiles * mixed, LANES), BF16),
            scratch_shapes=[pltpu.VMEM((2 * mixed, LANES), F32)],
            input_output_aliases={3: 0} if previous else {},
            compiler_params=params(),
            cost_estimate=cost(2 * count * tile * width * tile, 4 * count * tile * width),
        )(panel_all, w, mixed_rows(slab), *previous)

    def halve(value, exchange, bit):
        half = value.shape[0] // 2
        return value[:half].astype(F32) + exchange(value[half:], bit).astype(F32)

    def sum_all(values):
        values = [v.astype(F32) for v in values]
        while len(values) > 1:
            values = [values[i] + values[i + 1] for i in range(0, len(values), 2)]
        return values[0]

    def row_sum(value, bits):
        steps = [sum(b for k, b in enumerate(bits) if (q >> k) & 1) for q in range(1 << len(bits))]
        return sum_all([value] + [permute_row(value, step) for step in steps[1:]])

    col_bits, row_bits = list(reversed(bits_of(n_col))), list(reversed(bits_of(n_row)))
    some = tiles // 2
    e_part = halve(e_part, permute_row, 1).astype(BF16)
    gi = sum_all([gi[0]] + [permute_col(gi[q], q) for q in range(1, n_col)]).astype(BF16)
    h_low = h_part(0, half)
    e_part, gi, h_low, w, w_flip = lax.optimization_barrier((e_part, gi, h_low, w, w_flip))

    gi = row_sum(gi, row_bits[:1]).astype(BF16)
    h_low = halve(h_low, permute_col, 1).astype(BF16)
    h_high = h_part(half, tiles - half)
    e_part, gi, h_low, h_high, w = lax.optimization_barrier((e_part, gi, h_low, h_high, w))

    for bit in col_bits[1:]:
        e_part = halve(e_part, permute_row, bit).astype(BF16)
    h_high = halve(h_high, permute_col, 1).astype(BF16)
    gi = row_sum(gi, row_bits[1:2])
    for bit in col_bits[1:]:
        h_low = halve(h_low.astype(BF16), permute_col, bit)
    updated = update(0, some, [])
    e_part, gi, h_high, updated, w = lax.optimization_barrier((e_part, gi, h_high, updated, w))

    for bit in col_bits[1:]:
        h_high = halve(h_high.astype(BF16), permute_col, bit)
    e_own = sum_all([transpose(e_part[0, m], m, back=True) for m in range(groups)])
    for bit in row_bits[2:]:
        gi = row_sum(gi.astype(BF16), [bit])
    updated = update(some, tiles - some, [updated])
    h_low, h_high, e_own, gi, updated = lax.optimization_barrier((h_low, h_high, e_own, gi, updated))
    h = jnp.concatenate([h_low[0], h_high[0]], 0)
    grad_panel = jnp.concatenate([h[:slots] + e_own, h[slots:]], 0)
    updated = updated.reshape(tiles, tile, tile // LANES, slabs, LANES).transpose(0, 1, 3, 2, 4)
    return (
        updated.reshape(slab.shape),
        grad_panel.transpose(0, 2, 1).reshape(panel.shape),
        gi.T,
    )


def solution(mesh):
    in_specs = (
        P(None, "row", None, "col"),
        P(None, "row", None, None, "col", None),
        P(None, "row", None, None, "col", None),
        P(),
    )
    out_specs = (
        P(None, "row", None, None, "col", None),
        P(None, "row", None, "col"),
        P(None, "col"),
    )
    return jax.shard_map(
        per_device, mesh=mesh, in_specs=in_specs, out_specs=out_specs, check_vma=False
    )
```

profile of v0, /device:TPU:0, one launch (start us, length us, event | category | flops | bytes accessed | tf_op | source)
XLA Modules:
  0.0 54.7 jit_solution(14669438941105158977)
XLA Ops:
  0.6 1.1 %fusion.2.refs_0_ = bf16[8,64,256]{2,1,0:T(8,128)(2,1)S(1)} fusion(f32[8,1,256,64]{2,3,1,0:T(8,128)} %param.4), kind=kLoop, calls=%fused_computation.8 | loop fusion | flops 131072 | bytes 786432 | tf_op jit(solution)/shard_map/convert_element_type | solution.py:206
  2.3 2.6 %collective-permute-start.3 = (bf16[8,64,256]{2,1,0:T(8,128)(2,1)S(1)}, bf16[8,64,256]{2,1,0:T(8,128)(2,1)S(1)}, u32[]{:S(2)}, u32[]{:S(2)}) collective-permute-start(bf16[8,64,256]{2,1,0:T(8,128)(2,1)S(1)} %fusion.2.refs_0_), channel_id=1, source_target_pairs={{0,2},{1,3},{2,0},{3,1},{4,6},{5,7},{6,4},{7,5},{8,10},{9,11},{10,... | collective-permute-start | bytes 786440 | tf_op jit(solution)/shard_map/ppermute | solution.py:192
  4.8 1.6 %collective-permute-start = (bf16[2,64,256]{2,1,0:T(8,128)(2,1)S(1)}, bf16[2,64,256]{2,1,0:T(8,128)(2,1)S(1)}, u32[]{:S(2)}, u32[]{:S(2)}) collective-permute-start(bf16[2,64,256]{2,1,0:T(8,128)(2,1)S(1)} %slice.89), channel_id=1, source_target_pairs={{0,8},{1,12},{2,0},{3,4},{4,9},{5,13},{6,1},{7,5},{8,10},{9,14},{1... | collective-permute-start | bytes 196616 | tf_op jit(solution)/shard_map/ppermute | solution.py:204
  6.4 2.6 %collective-permute-start.1 = (bf16[2,64,256]{2,1,0:T(8,128)(2,1)S(1)}, bf16[2,64,256]{2,1,0:T(8,128)(2,1)S(1)}, u32[]{:S(2)}, u32[]{:S(2)}) collective-permute-start(bf16[2,64,256]{2,1,0:T(8,128)(2,1)S(1)} %slice.89), channel_id=1, source_target_pairs={{0,24},{1,28},{2,16},{3,20},{4,25},{5,29},{6,17},{7,21},{8,26},{9,... | collective-permute-start | bytes 196616 | tf_op jit(solution)/shard_map/ppermute | solution.py:204
  9.0 4.9 %shard_map.67 = (bf16[2048,1024]{1,0:T(8,128)(2,1)}, f32[8,128]{1,0:T(8,128)}) custom-call(bf16[16384,128]{1,0:T(8,128)(2,1)} %bitcast.54), custom_call_target="tpu_custom_call" | custom-call | bytes 8388608 | tf_op jit(solution)/shard_map/pallas_call | solution.py:213
  14.5 1.2 %collective-permute-start.4 = (bf16[8,64,256]{2,1,0:T(8,128)(2,1)S(1)}, bf16[8,64,256]{2,1,0:T(8,128)(2,1)S(1)}, u32[]{:S(2)}, u32[]{:S(2)}) collective-permute-start(bf16[8,64,256]{2,1,0:T(8,128)(2,1)S(1)} %collective-permute-done.3.refs_2_), channel_id=1, source_target_pairs={{0,1},{1,0},{2,3},{3,2},{4,5},{5,4},{6,7},{7,6},{8,9},{9,8},{10,11... | collective-permute-start | bytes 786440 | tf_op jit(solution)/shard_map/ppermute | solution.py:192
  15.7 0.6 %collective-permute-start.6 = (bf16[2,2,64,256]{3,2,1,0:T(8,128)(2,1)S(1)}, bf16[2,2,64,256]{3,2,1,0:T(8,128)(2,1)S(1)}, u32[]{:S(2)}, u32[]{:S(2)}) collective-permute-start(bf16[2,2,64,256]{3,2,1,0:T(8,128)(2,1)S(1)} %pad_maximum_fusion.1.refs_0_), channel_id=1, source_target_pairs={{0,4},{4,0},{8,12},{12,8},{16,20},{20,16},{24,28},{28,24},{1,5},{5... | collective-permute-start | bytes 393224 | tf_op jit(solution)/shard_map/ppermute | solution.py:189
  16.3 0.8 %collective-permute-start.7 = (bf16[2,2,64,256]{3,2,1,0:T(8,128)(2,1)S(1)}, bf16[2,2,64,256]{3,2,1,0:T(8,128)(2,1)S(1)}, u32[]{:S(2)}, u32[]{:S(2)}) collective-permute-start(bf16[2,2,64,256]{3,2,1,0:T(8,128)(2,1)S(1)} %pad_maximum_fusion.1.refs_0_), channel_id=1, source_target_pairs={{0,8},{4,12},{8,0},{12,4},{16,24},{20,28},{24,16},{28,20},{1,9},{5... | collective-permute-start | bytes 393224 | tf_op jit(solution)/shard_map/ppermute | solution.py:189
  17.1 2.1 %collective-permute-start.8 = (bf16[2,2,64,256]{3,2,1,0:T(8,128)(2,1)S(1)}, bf16[2,2,64,256]{3,2,1,0:T(8,128)(2,1)S(1)}, u32[]{:S(2)}, u32[]{:S(2)}) collective-permute-start(bf16[2,2,64,256]{3,2,1,0:T(8,128)(2,1)S(1)} %pad_maximum_fusion.1.refs_0_), channel_id=1, source_target_pairs={{0,12},{4,8},{8,4},{12,0},{16,28},{20,24},{24,20},{28,16},{1,13},{... | collective-permute-start | bytes 393224 | tf_op jit(solution)/shard_map/ppermute | solution.py:189
  19.3 4.2 %shard_map.68 = (bf16[4,256,256]{2,1,0:T(8,128)(2,1)S(1)}, bf16[4,2,2,64,256]{4,3,2,1,0:T(8,128)(2,1)S(1)}, bf16[256,2048]{1,0:T(8,128)(2,1)S(1)}, bf16[2,256,256]{2,1,0:T(8,128)(2,1)S(1)}) custom-call(s32[2]{0:T(128)S(1)} %pad_add_fusion.place_ref, bf16[8,64,256]{2,1,0:T(8,128)(2,1)S(1)} %fusion.2.refs_0_, ...), custom_call_target="tpu_custom_call" | custom-call | flops 1073741824 | bytes 5242880 | tf_op jit(solution)/shard_map/pallas_call | solution.py:242
  23.5 0.6 %collective-permute-start.5 = (bf16[2,2,2,64,256]{4,3,2,1,0:T(8,128)(2,1)S(1)}, bf16[2,2,2,64,256]{4,3,2,1,0:T(8,128)(2,1)S(1)}, u32[]{:S(2)}, u32[]{:S(2)}) collective-permute-start(bf16[2,2,2,64,256]{4,3,2,1,0:T(8,128)(2,1)S(1)} %slice.69), channel_id=1, source_target_pairs={{0,4},{4,0},{8,12},{12,8},{16,20},{20,16},{24,28},{28,24},{1,5},{5... | collective-permute-start | bytes 786440 | tf_op jit(solution)/shard_map/ppermute | solution.py:189
  24.1 1.1 %collective-permute-done.8.refs_3_ = bf16[2,2,64,256]{3,2,1,0:T(8,128)(2,1)S(1)} collective-permute-done((bf16[2,2,64,256]{3,2,1,0:T(8,128)(2,1)S(1)}, bf16[2,2,64,256]{3,2,1,0:T(8,128)(2,1)S(1)}, u32[]{:S(2)}, u32[]{:S(2)}) %collective-permute-start.8) | collective-permute-done | bytes 131104 | tf_op jit(solution)/shard_map/ppermute | solution.py:189
  25.2 1.7 %shard_map.69 = (bf16[256,1024]{1,0:T(8,128)(2,1)S(1)}, bf16[1024,256]{1,0:T(8,128)(2,1)S(1)}, bf16[4,64,256]{2,1,0:T(8,128)(2,1)S(1)}) custom-call(s32[2]{0:T(128)S(1)} %pad_add_fusion.place_ref, bf16[2,2,64,256]{3,2,1,0:T(8,128)(2,1)S(1)} %pad_maximum_fusion.1.refs_0_, bf16[2,2,64,256]{3,2,1,0:T(8,128)(2,1)S(1)} %collective-permute-done.6.refs_1_, ...), custom_call_target="tpu_custom_call" | custom-call | flops 256 | bytes 256 | tf_op jit(solution)/shard_map/pallas_call | solution.py:268
  26.9 1.4 %collective-permute-start.10 = (bf16[64,256]{1,0:T(8,128)(2,1)S(1)}, bf16[64,256]{1,0:T(8,128)(2,1)S(1)}, u32[]{:S(2)}, u32[]{:S(2)}) collective-permute-start(bf16[64,256]{1,0:T(8,128)(2,1)S(1)} %get-tuple-element.80), channel_id=1, source_target_pairs={{0,2},{1,3},{2,0},{3,1},{4,6},{5,7},{6,4},{7,5},{8,10},{9,11},{10,... | collective-permute-start | bytes 98312 | tf_op jit(solution)/shard_map/ppermute | solution.py:192
  28.3 0.8 %collective-permute-start.9 = (bf16[64,256]{1,0:T(8,128)(2,1)S(1)}, bf16[64,256]{1,0:T(8,128)(2,1)S(1)}, u32[]{:S(2)}, u32[]{:S(2)}) collective-permute-start(bf16[64,256]{1,0:T(8,128)(2,1)S(1)} %get-tuple-element.78), channel_id=1, source_target_pairs={{0,1},{1,0},{2,3},{3,2},{4,5},{5,4},{6,7},{7,6},{8,9},{9,8},{10,11... | collective-permute-start | bytes 98312 | tf_op jit(solution)/shard_map/ppermute | solution.py:192
  29.1 1.6 %shard_map.70 = bf16[4,4,64,256]{3,2,1,0:T(8,128)(2,1)S(1)} custom-call(s32[2]{0:T(128)S(1)} %pad_add_fusion.place_ref, bf16[1024,256]{1,0:T(8,128)(2,1)S(1)} %get-tuple-element.55.wt_ref, bf16[2048,1024]{1,0:T(8,128)(2,1)S(1)} %copy-done), custom_call_target="tpu_custom_call" | custom-call | flops 256 | bytes 256 | tf_op jit(solution)/shard_map/pallas_call | solution.py:283
  30.9 0.8 %collective-permute-done.11 = bf16[64,256]{1,0:T(8,128)(2,1)S(1)} collective-permute-done((bf16[64,256]{1,0:T(8,128)(2,1)S(1)}, bf16[64,256]{1,0:T(8,128)(2,1)S(1)}, u32[]{:S(2)}, u32[]{:S(2)}) %collective-permute-start.11) | collective-permute-done | bytes 32800 | tf_op jit(solution)/shard_map/ppermute | solution.py:192
  31.9 1.2 %collective-permute-start.12 = (bf16[64,256]{1,0:T(8,128)(2,1)S(1)}, bf16[64,256]{1,0:T(8,128)(2,1)S(1)}, u32[]{:S(2)}, u32[]{:S(2)}) collective-permute-start(bf16[64,256]{1,0:T(8,128)(2,1)S(1)} %fusion.4), channel_id=1, source_target_pairs={{0,4},{4,0},{8,12},{12,8},{16,20},{20,16},{24,28},{28,24},{1,5},{5... | collective-permute-start | bytes 98312 | tf_op jit(solution)/shard_map/ppermute | solution.py:189
  33.1 1.6 %shard_map.71 = bf16[4,4,64,256]{3,2,1,0:T(8,128)(2,1)S(1)} custom-call(s32[2]{0:T(128)S(1)} %pad_add_fusion.place_ref, bf16[1024,256]{1,0:T(8,128)(2,1)S(1)} %get-tuple-element.55.wt_ref, bf16[2048,1024]{1,0:T(8,128)(2,1)S(1)} %copy-done), custom_call_target="tpu_custom_call" | custom-call | flops 256 | bytes 256 | tf_op jit(solution)/shard_map/pallas_call | solution.py:283
  34.7 1.2 %collective-permute-done.12 = bf16[64,256]{1,0:T(8,128)(2,1)S(1)} collective-permute-done((bf16[64,256]{1,0:T(8,128)(2,1)S(1)}, bf16[64,256]{1,0:T(8,128)(2,1)S(1)}, u32[]{:S(2)}, u32[]{:S(2)}) %collective-permute-start.12) | collective-permute-done | bytes 32800 | tf_op jit(solution)/shard_map/ppermute | solution.py:189
  36.0 1.8 %collective-permute-start.16 = (bf16[64,256]{1,0:T(8,128)(2,1)S(1)}, bf16[64,256]{1,0:T(8,128)(2,1)S(1)}, u32[]{:S(2)}, u32[]{:S(2)}) collective-permute-start(bf16[64,256]{1,0:T(8,128)(2,1)S(1)} %add_convert_fusion.4), channel_id=1, source_target_pairs={{0,8},{4,12},{8,0},{12,4},{16,24},{20,28},{24,16},{28,20},{1,9},{5... | collective-permute-start | bytes 98312 | tf_op jit(solution)/shard_map/ppermute | solution.py:189
  38.2 1.2 %collective-permute-start.14 = (bf16[1,4,64,256]{3,2,1,0:T(8,128)(2,1)S(1)}, bf16[1,4,64,256]{3,2,1,0:T(8,128)(2,1)S(1)}, u32[]{:S(2)}, u32[]{:S(2)}) collective-permute-start(bf16[1,4,64,256]{3,2,1,0:T(8,128)(2,1)S(1)} %slice.77), channel_id=1, source_target_pairs={{0,2},{1,3},{2,0},{3,1},{4,6},{5,7},{6,4},{7,5},{8,10},{9,11},{10,... | collective-permute-start | bytes 393224 | tf_op jit(solution)/shard_map/ppermute | solution.py:192
  39.4 2.4 %shard_map.72.refs_0_ = bf16[16384,128]{1,0:T(8,128)(2,1)} custom-call(bf16[256,2048]{1,0:T(8,128)(2,1)S(1)} %get-tuple-element.61.pt_ref, bf16[256,1024]{1,0:T(8,128)(2,1)S(1)} %get-tuple-element.66.w_ref, bf16[16384,128]{1,0:T(8,128)(2,1)S(1)} %bitcast.51), custom_call_target="tpu_custom_call" | custom-call | flops 536870912 | bytes 4194304 | tf_op jit(solution)/shard_map/pallas_call | solution.py:298
  41.8 1.7 %collective-permute-done.15 = bf16[1,2,2,64,256]{4,3,2,1,0:T(8,128)(2,1)S(1)} collective-permute-done((bf16[1,2,2,64,256]{4,3,2,1,0:T(8,128)(2,1)S(1)}, bf16[1,2,2,64,256]{4,3,2,1,0:T(8,128)(2,1)S(1)}, u32[]{:S(2)}, u32[]{:S(2)}) %collective-permute-start.15) | collective-permute-done | bytes 131104 | tf_op jit(solution)/shard_map/ppermute | solution.py:189
  43.7 2.7 %collective-permute-start.21 = (bf16[64,256]{1,0:T(8,128)(2,1)S(1)}, bf16[64,256]{1,0:T(8,128)(2,1)S(1)}, u32[]{:S(2)}, u32[]{:S(2)}) collective-permute-start(bf16[64,256]{1,0:T(8,128)(2,1)S(1)} %convert_add_fusion.5), channel_id=1, source_target_pairs={{0,16},{4,20},{8,24},{12,28},{16,0},{20,4},{24,8},{28,12},{1,17},{... | collective-permute-start | bytes 98312 | tf_op jit(solution)/shard_map/ppermute | solution.py:189
  46.4 1.2 %collective-permute-start.19 = (bf16[2,64,256]{2,1,0:T(8,128)(2,1)S(1)}, bf16[2,64,256]{2,1,0:T(8,128)(2,1)S(1)}, u32[]{:S(2)}, u32[]{:S(2)}) collective-permute-start(bf16[2,64,256]{2,1,0:T(8,128)(2,1)S(1)} %get-tuple-element.76), channel_id=1, source_target_pairs={{8,0},{12,1},{0,2},{4,3},{9,4},{13,5},{1,6},{5,7},{10,8},{14,9},{2... | collective-permute-start | bytes 196616 | tf_op jit(solution)/shard_map/ppermute | solution.py:204
  47.5 1.1 %collective-permute-start.20 = (bf16[2,64,256]{2,1,0:T(8,128)(2,1)S(1)}, bf16[2,64,256]{2,1,0:T(8,128)(2,1)S(1)}, u32[]{:S(2)}, u32[]{:S(2)}) collective-permute-start(bf16[2,64,256]{2,1,0:T(8,128)(2,1)S(1)} %get-tuple-element.77), channel_id=1, source_target_pairs={{24,0},{28,1},{16,2},{20,3},{25,4},{29,5},{17,6},{21,7},{26,8},{30... | collective-permute-start | bytes 196616 | tf_op jit(solution)/shard_map/ppermute | solution.py:204
  48.7 1.4 %collective-permute-start.18 = (bf16[1,4,64,256]{3,2,1,0:T(8,128)(2,1)S(1)}, bf16[1,4,64,256]{3,2,1,0:T(8,128)(2,1)S(1)}, u32[]{:S(2)}, u32[]{:S(2)}) collective-permute-start(bf16[1,4,64,256]{3,2,1,0:T(8,128)(2,1)S(1)} %slice.83), channel_id=1, source_target_pairs={{0,2},{1,3},{2,0},{3,1},{4,6},{5,7},{6,4},{7,5},{8,10},{9,11},{10,... | collective-permute-start | bytes 393224 | tf_op jit(solution)/shard_map/ppermute | solution.py:192
  50.0 2.4 %shard_map.73 = bf16[16384,128]{1,0:T(8,128)(2,1)} custom-call(bf16[256,2048]{1,0:T(8,128)(2,1)S(1)} %get-tuple-element.61.pt_ref, bf16[256,1024]{1,0:T(8,128)(2,1)S(1)} %get-tuple-element.66.w_ref, bf16[16384,128]{1,0:T(8,128)(2,1)S(1)} %bitcast.52, bf16[16384,128]{1,0:T(8,128)(2,1)} %shard_map.72.refs_0_), custom_call_target="tpu_custom_call", output_to_operand_aliasing={{}: (3, {})} | custom-call | flops 536870912 | bytes 4194304 | tf_op jit(solution)/shard_map/pallas_call | solution.py:298
  52.4 0.6 %convert_add_fusion.4 = f32[64,256]{1,0:T(8,128)} fusion(bf16[64,256]{1,0:T(8,128)(2,1)S(1)} %collective-permute-done.21, bf16[64,256]{1,0:T(8,128)(2,1)S(1)} %convert_add_fusion.5), kind=kLoop, calls=%fused_computation.18 | loop fusion | flops 49152 | bytes 131072 | tf_op jit(solution)/shard_map/add | solution.py:322
  53.1 0.6 %collective-permute-done.20 = bf16[2,64,256]{2,1,0:T(8,128)(2,1)S(1)} collective-permute-done((bf16[2,64,256]{2,1,0:T(8,128)(2,1)S(1)}, bf16[2,64,256]{2,1,0:T(8,128)(2,1)S(1)}, u32[]{:S(2)}, u32[]{:S(2)}) %collective-permute-start.20) | collective-permute-done | bytes 65568 | tf_op jit(solution)/shard_map/ppermute | solution.py:204
  53.9 0.8 %fusion.1 = f32[8,1,256,64]{2,3,1,0:T(8,128)} fusion(f32[4,64,256]{2,1,0:T(8,128)S(1)} %bitcast.56, f32[4,64,256]{2,1,0:T(8,128)S(1)} %bitcast.55, f32[2,64,256]{2,1,0:T(8,128)S(1)} %bitcast_add_fusion), kind=kLoop, calls=%fused_computation.2 | loop fusion | flops 524288 | bytes 1179648
  (52 shorter events, 2.5 us)
Async XLA Ops:
  0.6 18.7 %copy-start.2 = (f32[256,256]{1,0:T(8,128)S(1)}, f32[256,256]{1,0:T(8,128)}, u32[]{:S(2)}) copy-start(f32[256,256]{1,0:T(8,128)} %refs_5_.1) | copy-start | bytes 786436
  1.8 12.7 %collective-permute-start.2 = (bf16[8,64,256]{2,1,0:T(8,128)(2,1)S(1)}, bf16[8,64,256]{2,1,0:T(8,128)(2,1)S(1)}, u32[]{:S(2)}, u32[]{:S(2)}) collective-permute-start(bf16[8,64,256]{2,1,0:T(8,128)(2,1)S(1)} %fusion.2.refs_0_), channel_id=1, source_target_pairs={{0,1},{1,0},{2,3},{3,2},{4,5},{5,4},{6,7},{7,6},{8,9},{9,8},{10,11... | collective-permute-start | bytes 786440 | tf_op jit(solution)/shard_map/ppermute | solution.py:192
  2.3 12.2 %collective-permute-start.3 = (bf16[8,64,256]{2,1,0:T(8,128)(2,1)S(1)}, bf16[8,64,256]{2,1,0:T(8,128)(2,1)S(1)}, u32[]{:S(2)}, u32[]{:S(2)}) collective-permute-start(bf16[8,64,256]{2,1,0:T(8,128)(2,1)S(1)} %fusion.2.refs_0_), channel_id=1, source_target_pairs={{0,2},{1,3},{2,0},{3,1},{4,6},{5,7},{6,4},{7,5},{8,10},{9,11},{10,... | collective-permute-start | bytes 786440 | tf_op jit(solution)/shard_map/ppermute | solution.py:192
  4.8 9.1 %collective-permute-start = (bf16[2,64,256]{2,1,0:T(8,128)(2,1)S(1)}, bf16[2,64,256]{2,1,0:T(8,128)(2,1)S(1)}, u32[]{:S(2)}, u32[]{:S(2)}) collective-permute-start(bf16[2,64,256]{2,1,0:T(8,128)(2,1)S(1)} %slice.89), channel_id=1, source_target_pairs={{0,8},{1,12},{2,0},{3,4},{4,9},{5,13},{6,1},{7,5},{8,10},{9,14},{1... | collective-permute-start | bytes 196616 | tf_op jit(solution)/shard_map/ppermute | solution.py:204
  6.4 8.1 %collective-permute-start.1 = (bf16[2,64,256]{2,1,0:T(8,128)(2,1)S(1)}, bf16[2,64,256]{2,1,0:T(8,128)(2,1)S(1)}, u32[]{:S(2)}, u32[]{:S(2)}) collective-permute-start(bf16[2,64,256]{2,1,0:T(8,128)(2,1)S(1)} %slice.89), channel_id=1, source_target_pairs={{0,24},{1,28},{2,16},{3,20},{4,25},{5,29},{6,17},{7,21},{8,26},{9,... | collective-permute-start | bytes 196616 | tf_op jit(solution)/shard_map/ppermute | solution.py:204
  13.9 11.3 %copy-start.3 = (f32[8,128]{1,0:T(8,128)S(1)}, f32[8,128]{1,0:T(8,128)}, u32[]{:S(2)}) copy-start(f32[8,128]{1,0:T(8,128)} %get-tuple-element.48.refs_7_) | copy-start | bytes 12292
  14.5 4.8 %collective-permute-start.4 = (bf16[8,64,256]{2,1,0:T(8,128)(2,1)S(1)}, bf16[8,64,256]{2,1,0:T(8,128)(2,1)S(1)}, u32[]{:S(2)}, u32[]{:S(2)}) collective-permute-start(bf16[8,64,256]{2,1,0:T(8,128)(2,1)S(1)} %collective-permute-done.3.refs_2_), channel_id=1, source_target_pairs={{0,1},{1,0},{2,3},{3,2},{4,5},{5,4},{6,7},{7,6},{8,9},{9,8},{10,11... | collective-permute-start | bytes 786440 | tf_op jit(solution)/shard_map/ppermute | solution.py:192
  15.7 13.4 %copy-start = (bf16[2048,1024]{1,0:T(8,128)(2,1)S(1)}, bf16[2048,1024]{1,0:T(8,128)(2,1)}, u32[]{:S(2)}) copy-start(bf16[2048,1024]{1,0:T(8,128)(2,1)} %get-tuple-element.42.refs_5_.g_ref) | copy-start | bytes 12582916
  15.7 8.4 %collective-permute-start.6 = (bf16[2,2,64,256]{3,2,1,0:T(8,128)(2,1)S(1)}, bf16[2,2,64,256]{3,2,1,0:T(8,128)(2,1)S(1)}, u32[]{:S(2)}, u32[]{:S(2)}) collective-permute-start(bf16[2,2,64,256]{3,2,1,0:T(8,128)(2,1)S(1)} %pad_maximum_fusion.1.refs_0_), channel_id=1, source_target_pairs={{0,4},{4,0},{8,12},{12,8},{16,20},{20,16},{24,28},{28,24},{1,5},{5... | collective-permute-start | bytes 393224 | tf_op jit(solution)/shard_map/ppermute | solution.py:189
  16.3 7.8 %collective-permute-start.7 = (bf16[2,2,64,256]{3,2,1,0:T(8,128)(2,1)S(1)}, bf16[2,2,64,256]{3,2,1,0:T(8,128)(2,1)S(1)}, u32[]{:S(2)}, u32[]{:S(2)}) collective-permute-start(bf16[2,2,64,256]{3,2,1,0:T(8,128)(2,1)S(1)} %pad_maximum_fusion.1.refs_0_), channel_id=1, source_target_pairs={{0,8},{4,12},{8,0},{12,4},{16,24},{20,28},{24,16},{28,20},{1,9},{5... | collective-permute-start | bytes 393224 | tf_op jit(solution)/shard_map/ppermute | solution.py:189
  17.1 8.1 %collective-permute-start.8 = (bf16[2,2,64,256]{3,2,1,0:T(8,128)(2,1)S(1)}, bf16[2,2,64,256]{3,2,1,0:T(8,128)(2,1)S(1)}, u32[]{:S(2)}, u32[]{:S(2)}) collective-permute-start(bf16[2,2,64,256]{3,2,1,0:T(8,128)(2,1)S(1)} %pad_maximum_fusion.1.refs_0_), channel_id=1, source_target_pairs={{0,12},{4,8},{8,4},{12,0},{16,28},{20,24},{24,20},{28,16},{1,13},{... | collective-permute-start | bytes 393224 | tf_op jit(solution)/shard_map/ppermute | solution.py:189
  23.5 8.2 %collective-permute-start.5 = (bf16[2,2,2,64,256]{4,3,2,1,0:T(8,128)(2,1)S(1)}, bf16[2,2,2,64,256]{4,3,2,1,0:T(8,128)(2,1)S(1)}, u32[]{:S(2)}, u32[]{:S(2)}) collective-permute-start(bf16[2,2,2,64,256]{4,3,2,1,0:T(8,128)(2,1)S(1)} %slice.69), channel_id=1, source_target_pairs={{0,4},{4,0},{8,12},{12,8},{16,20},{20,16},{24,28},{28,24},{1,5},{5... | collective-permute-start | bytes 786440 | tf_op jit(solution)/shard_map/ppermute | solution.py:189
  26.9 4.0 %collective-permute-start.10 = (bf16[64,256]{1,0:T(8,128)(2,1)S(1)}, bf16[64,256]{1,0:T(8,128)(2,1)S(1)}, u32[]{:S(2)}, u32[]{:S(2)}) collective-permute-start(bf16[64,256]{1,0:T(8,128)(2,1)S(1)} %get-tuple-element.80), channel_id=1, source_target_pairs={{0,2},{1,3},{2,0},{3,1},{4,6},{5,7},{6,4},{7,5},{8,10},{9,11},{10,... | collective-permute-start | bytes 98312 | tf_op jit(solution)/shard_map/ppermute | solution.py:192
  28.3 3.3 %collective-permute-start.11 = (bf16[64,256]{1,0:T(8,128)(2,1)S(1)}, bf16[64,256]{1,0:T(8,128)(2,1)S(1)}, u32[]{:S(2)}, u32[]{:S(2)}) collective-permute-start(bf16[64,256]{1,0:T(8,128)(2,1)S(1)} %get-tuple-element.79), channel_id=1, source_target_pairs={{0,3},{1,2},{2,1},{3,0},{4,7},{5,6},{6,5},{7,4},{8,11},{9,10},{10,... | collective-permute-start | bytes 98312 | tf_op jit(solution)/shard_map/ppermute | solution.py:192
  28.3 3.3 %collective-permute-start.9 = (bf16[64,256]{1,0:T(8,128)(2,1)S(1)}, bf16[64,256]{1,0:T(8,128)(2,1)S(1)}, u32[]{:S(2)}, u32[]{:S(2)}) collective-permute-start(bf16[64,256]{1,0:T(8,128)(2,1)S(1)} %get-tuple-element.78), channel_id=1, source_target_pairs={{0,1},{1,0},{2,3},{3,2},{4,5},{5,4},{6,7},{7,6},{8,9},{9,8},{10,11... | collective-permute-start | bytes 98312 | tf_op jit(solution)/shard_map/ppermute | solution.py:192
  31.7 7.8 %copy-start.1 = (bf16[8,1,256,4,1,256]{5,3,4,2,1,0:T(4,128)(2,1)S(1)}, bf16[8,1,256,4,1,256]{5,3,4,2,1,0:T(4,128)(2,1)}, u32[]{:S(2)}) copy-start(bf16[8,1,256,4,1,256]{5,3,4,2,1,0:T(4,128)(2,1)} %param.5) | copy-start | bytes 12582916
  31.8 4.1 %collective-permute-start.13 = (bf16[2,4,64,256]{3,2,1,0:T(8,128)(2,1)S(1)}, bf16[2,4,64,256]{3,2,1,0:T(8,128)(2,1)S(1)}, u32[]{:S(2)}, u32[]{:S(2)}) collective-permute-start(bf16[2,4,64,256]{3,2,1,0:T(8,128)(2,1)S(1)} %slice.75), channel_id=1, source_target_pairs={{0,1},{1,0},{2,3},{3,2},{4,5},{5,4},{6,7},{7,6},{8,9},{9,8},{10,11... | collective-permute-start | bytes 786440 | tf_op jit(solution)/shard_map/ppermute | solution.py:192
  31.9 4.0 %collective-permute-start.12 = (bf16[64,256]{1,0:T(8,128)(2,1)S(1)}, bf16[64,256]{1,0:T(8,128)(2,1)S(1)}, u32[]{:S(2)}, u32[]{:S(2)}) collective-permute-start(bf16[64,256]{1,0:T(8,128)(2,1)S(1)} %fusion.4), channel_id=1, source_target_pairs={{0,4},{4,0},{8,12},{12,8},{16,20},{20,16},{24,28},{28,24},{1,5},{5... | collective-permute-start | bytes 98312 | tf_op jit(solution)/shard_map/ppermute | solution.py:189
  36.0 7.7 %collective-permute-start.17 = (bf16[2,4,64,256]{3,2,1,0:T(8,128)(2,1)S(1)}, bf16[2,4,64,256]{3,2,1,0:T(8,128)(2,1)S(1)}, u32[]{:S(2)}, u32[]{:S(2)}) collective-permute-start(bf16[2,4,64,256]{3,2,1,0:T(8,128)(2,1)S(1)} %slice.81), channel_id=1, source_target_pairs={{0,1},{1,0},{2,3},{3,2},{4,5},{5,4},{6,7},{7,6},{8,9},{9,8},{10,11... | collective-permute-start | bytes 786440 | tf_op jit(solution)/shard_map/ppermute | solution.py:192
  36.0 5.8 %collective-permute-start.16 = (bf16[64,256]{1,0:T(8,128)(2,1)S(1)}, bf16[64,256]{1,0:T(8,128)(2,1)S(1)}, u32[]{:S(2)}, u32[]{:S(2)}) collective-permute-start(bf16[64,256]{1,0:T(8,128)(2,1)S(1)} %add_convert_fusion.4), channel_id=1, source_target_pairs={{0,8},{4,12},{8,0},{12,4},{16,24},{20,28},{24,16},{28,20},{1,9},{5... | collective-permute-start | bytes 98312 | tf_op jit(solution)/shard_map/ppermute | solution.py:189
  37.9 5.6 %collective-permute-start.15 = (bf16[1,2,2,64,256]{4,3,2,1,0:T(8,128)(2,1)S(1)}, bf16[1,2,2,64,256]{4,3,2,1,0:T(8,128)(2,1)S(1)}, u32[]{:S(2)}, u32[]{:S(2)}) collective-permute-start(bf16[1,2,2,64,256]{4,3,2,1,0:T(8,128)(2,1)S(1)} %slice.79), channel_id=1, source_target_pairs={{0,8},{4,12},{8,0},{12,4},{16,24},{20,28},{24,16},{28,20},{1,9},{5... | collective-permute-start | bytes 393224 | tf_op jit(solution)/shard_map/ppermute | solution.py:189
  38.2 5.4 %collective-permute-start.14 = (bf16[1,4,64,256]{3,2,1,0:T(8,128)(2,1)S(1)}, bf16[1,4,64,256]{3,2,1,0:T(8,128)(2,1)S(1)}, u32[]{:S(2)}, u32[]{:S(2)}) collective-permute-start(bf16[1,4,64,256]{3,2,1,0:T(8,128)(2,1)S(1)} %slice.77), channel_id=1, source_target_pairs={{0,2},{1,3},{2,0},{3,1},{4,6},{5,7},{6,4},{7,5},{8,10},{9,11},{10,... | collective-permute-start | bytes 393224 | tf_op jit(solution)/shard_map/ppermute | solution.py:192
  43.7 8.7 %collective-permute-start.21 = (bf16[64,256]{1,0:T(8,128)(2,1)S(1)}, bf16[64,256]{1,0:T(8,128)(2,1)S(1)}, u32[]{:S(2)}, u32[]{:S(2)}) collective-permute-start(bf16[64,256]{1,0:T(8,128)(2,1)S(1)} %convert_add_fusion.5), channel_id=1, source_target_pairs={{0,16},{4,20},{8,24},{12,28},{16,0},{20,4},{24,8},{28,12},{1,17},{... | collective-permute-start | bytes 98312 | tf_op jit(solution)/shard_map/ppermute | solution.py:189
  46.4 6.7 %collective-permute-start.19 = (bf16[2,64,256]{2,1,0:T(8,128)(2,1)S(1)}, bf16[2,64,256]{2,1,0:T(8,128)(2,1)S(1)}, u32[]{:S(2)}, u32[]{:S(2)}) collective-permute-start(bf16[2,64,256]{2,1,0:T(8,128)(2,1)S(1)} %get-tuple-element.76), channel_id=1, source_target_pairs={{8,0},{12,1},{0,2},{4,3},{9,4},{13,5},{1,6},{5,7},{10,8},{14,9},{2... | collective-permute-start | bytes 196616 | tf_op jit(solution)/shard_map/ppermute | solution.py:204
  47.5 6.2 %collective-permute-start.20 = (bf16[2,64,256]{2,1,0:T(8,128)(2,1)S(1)}, bf16[2,64,256]{2,1,0:T(8,128)(2,1)S(1)}, u32[]{:S(2)}, u32[]{:S(2)}) collective-permute-start(bf16[2,64,256]{2,1,0:T(8,128)(2,1)S(1)} %get-tuple-element.77), channel_id=1, source_target_pairs={{24,0},{28,1},{16,2},{20,3},{25,4},{29,5},{17,6},{21,7},{26,8},{30... | collective-permute-start | bytes 196616 | tf_op jit(solution)/shard_map/ppermute | solution.py:204
  48.7 5.2 %collective-permute-start.18 = (bf16[1,4,64,256]{3,2,1,0:T(8,128)(2,1)S(1)}, bf16[1,4,64,256]{3,2,1,0:T(8,128)(2,1)S(1)}, u32[]{:S(2)}, u32[]{:S(2)}) collective-permute-start(bf16[1,4,64,256]{3,2,1,0:T(8,128)(2,1)S(1)} %slice.83), channel_id=1, source_target_pairs={{0,2},{1,3},{2,0},{3,1},{4,6},{5,7},{6,4},{7,5},{8,10},{9,11},{10,... | collective-permute-start | bytes 393224 | tf_op jit(solution)/shard_map/ppermute | solution.py:192
where the time goes:
time: 54.9 us; the launch traced here: 54.7 us
  starting transfers between devices  25.7 us (47%)
  Pallas kernels  18.8 us (34%)
  waiting for transfers between devices  6.18 us (11%)
  other arithmetic  3.05 us (6%)
  between operations  0.86 us (2%)
    ppermute x8, starting transfers between devices, permute_row(): return lax.ppermute(value, 'row', [(i, i ^ bit) for i in range(n_row)])  10.2 us
    ppermute x10, starting transfers between devices, permute_col(): return lax.ppermute(value, 'col', [(i, i ^ bit) for i in range(n_col)])  9.14 us
    ppermute x4, starting transfers between devices, transpose(): return lax.ppermute(value, BOTH, pairs)  6.41 us
    pallas_call x1, Pallas kernels, per_device(): pl.pallas_call(functools.partial(unmix_kernel, slabs, tile), grid=(tiles,...  4.92 us
    pallas_call x2, Pallas kernels, update(): pl.pallas_call(functools.partial(update_kernel, slabs, tile), grid=(count...  4.82 us
    pallas_call x1, Pallas kernels, per_device(): pl.pallas_call(functools.partial(q_kernel, n_row, n_col, groups), grid=(s...  4.16 us
    ppermute x8, waiting for transfers between devices, permute_row(): return lax.ppermute(value, 'row', [(i, i ^ bit) for i in range(n_row)])  3.89 us
    pallas_call x2, Pallas kernels, h_part(): pl.pallas_call(functools.partial(h_kernel, n_col), grid=(count // 2,), in...  3.2 us
  transfers between devices with their start and end apart: 22, of which 9 were waited for; matrix products, arithmetic and copies ran while one was open for 2% of the time, Pallas kernels for 34%

commit v1 on v0

--- a/solution.py
+++ b/solution.py
@@ -327,7 +327,7 @@
         return sum_all([value] + [permute_row(value, step) for step in steps[1:]])
 
     col_bits, row_bits = list(reversed(bits_of(n_col))), list(reversed(bits_of(n_row)))
-    some = tiles // 2
+    some = tiles * 3 // 4
     e_part = halve(e_part, permute_row, 1).astype(BF16)
     gi = sum_all([gi[0]] + [permute_col(gi[q], q) for q in range(1, n_col)]).astype(BF16)
     h_low = h_part(0, half)

time: 54.9 us -> 54.9 us (level)
    ppermute x8, waiting for transfers between devices: 3.89 us -> 2.93 us  [permute_row(): return lax.ppermute(value, 'row', [(i, i ^ bit) for i in range(n_row)])]
    ppermute x4, waiting for transfers between devices: 1.18 us -> 1.9 us  [transpose(): return lax.ppermute(value, BOTH, pairs)]
  transfers between devices with their start and end apart: 22 -> 22, of which waited for: 9 -> 9; matrix products, arithmetic and copies ran while one was open for 2% -> 2% of each run, Pallas kernels for 34% -> 35%
where the time goes in v1:
time: 54.9 us; the launch traced here: 54.7 us
  starting transfers between devices  25.7 us (47%)
  Pallas kernels  19 us (35%)
  waiting for transfers between devices  5.94 us (11%)
  other arithmetic  3.05 us (6%)
  between operations  0.86 us (2%)
    ppermute x8, starting transfers between devices, permute_row(): return lax.ppermute(value, 'row', [(i, i ^ bit) for i in range(n_row)])  10.2 us
    ppermute x10, starting transfers between devices, permute_col(): return lax.ppermute(value, 'col', [(i, i ^ bit) for i in range(n_col)])  9.14 us
    ppermute x4, starting transfers between devices, transpose(): return lax.ppermute(value, BOTH, pairs)  6.41 us
    pallas_call x2, Pallas kernels, update(): pl.pallas_call(functools.partial(update_kernel, slabs, tile), grid=(count...  5.05 us
    pallas_call x1, Pallas kernels, per_device(): pl.pallas_call(functools.partial(unmix_kernel, slabs, tile), grid=(tiles,...  4.92 us
    pallas_call x1, Pallas kernels, per_device(): pl.pallas_call(functools.partial(q_kernel, n_row, n_col, groups), grid=(s...  4.16 us
    pallas_call x2, Pallas kernels, h_part(): pl.pallas_call(functools.partial(h_kernel, n_col), grid=(count // 2,), in...  3.2 us
    ppermute x8, waiting for transfers between devices, permute_row(): return lax.ppermute(value, 'row', [(i, i ^ bit) for i in range(n_row)])  2.93 us
  transfers between devices with their start and end apart: 22, of which 9 were waited for; matrix products, arithmetic and copies ran while one was open for 2% of the time, Pallas kernels for 35%

profile of v1, /device:TPU:0, one launch (start us, length us, event | category | flops | bytes accessed | tf_op | source)
XLA Modules:
  0.0 54.7 jit_solution(1156096479224531613)
XLA Ops:
  0.6 1.1 %fusion.2.refs_0_ = bf16[8,64,256]{2,1,0:T(8,128)(2,1)S(1)} fusion(f32[8,1,256,64]{2,3,1,0:T(8,128)} %param.4), kind=kLoop, calls=%fused_computation.8 | loop fusion | flops 131072 | bytes 786432 | tf_op jit(solution)/shard_map/convert_element_type | solution.py:206
  2.3 2.6 %collective-permute-start.3 = (bf16[8,64,256]{2,1,0:T(8,128)(2,1)S(1)}, bf16[8,64,256]{2,1,0:T(8,128)(2,1)S(1)}, u32[]{:S(2)}, u32[]{:S(2)}) collective-permute-start(bf16[8,64,256]{2,1,0:T(8,128)(2,1)S(1)} %fusion.2.refs_0_), channel_id=1, source_target_pairs={{0,2},{1,3},{2,0},{3,1},{4,6},{5,7},{6,4},{7,5},{8,10},{9,11},{10,... | collective-permute-start | bytes 786440 | tf_op jit(solution)/shard_map/ppermute | solution.py:192
  4.8 1.6 %collective-permute-start = (bf16[2,64,256]{2,1,0:T(8,128)(2,1)S(1)}, bf16[2,64,256]{2,1,0:T(8,128)(2,1)S(1)}, u32[]{:S(2)}, u32[]{:S(2)}) collective-permute-start(bf16[2,64,256]{2,1,0:T(8,128)(2,1)S(1)} %slice.89), channel_id=1, source_target_pairs={{0,8},{1,12},{2,0},{3,4},{4,9},{5,13},{6,1},{7,5},{8,10},{9,14},{1... | collective-permute-start | bytes 196616 | tf_op jit(solution)/shard_map/ppermute | solution.py:204
  6.4 2.6 %collective-permute-start.1 = (bf16[2,64,256]{2,1,0:T(8,128)(2,1)S(1)}, bf16[2,64,256]{2,1,0:T(8,128)(2,1)S(1)}, u32[]{:S(2)}, u32[]{:S(2)}) collective-permute-start(bf16[2,64,256]{2,1,0:T(8,128)(2,1)S(1)} %slice.89), channel_id=1, source_target_pairs={{0,24},{1,28},{2,16},{3,20},{4,25},{5,29},{6,17},{7,21},{8,26},{9,... | collective-permute-start | bytes 196616 | tf_op jit(solution)/shard_map/ppermute | solution.py:204
  9.0 4.9 %shard_map.67 = (bf16[2048,1024]{1,0:T(8,128)(2,1)}, f32[8,128]{1,0:T(8,128)}) custom-call(bf16[16384,128]{1,0:T(8,128)(2,1)} %bitcast.54), custom_call_target="tpu_custom_call" | custom-call | bytes 8388608 | tf_op jit(solution)/shard_map/pallas_call | solution.py:213
  14.5 1.2 %collective-permute-start.4 = (bf16[8,64,256]{2,1,0:T(8,128)(2,1)S(1)}, bf16[8,64,256]{2,1,0:T(8,128)(2,1)S(1)}, u32[]{:S(2)}, u32[]{:S(2)}) collective-permute-start(bf16[8,64,256]{2,1,0:T(8,128)(2,1)S(1)} %collective-permute-done.3.refs_2_), channel_id=1, source_target_pairs={{0,1},{1,0},{2,3},{3,2},{4,5},{5,4},{6,7},{7,6},{8,9},{9,8},{10,11... | collective-permute-start | bytes 786440 | tf_op jit(solution)/shard_map/ppermute | solution.py:192
  15.7 0.6 %collective-permute-start.6 = (bf16[2,2,64,256]{3,2,1,0:T(8,128)(2,1)S(1)}, bf16[2,2,64,256]{3,2,1,0:T(8,128)(2,1)S(1)}, u32[]{:S(2)}, u32[]{:S(2)}) collective-permute-start(bf16[2,2,64,256]{3,2,1,0:T(8,128)(2,1)S(1)} %pad_maximum_fusion.1.refs_0_), channel_id=1, source_target_pairs={{0,4},{4,0},{8,12},{12,8},{16,20},{20,16},{24,28},{28,24},{1,5},{5... | collective-permute-start | bytes 393224 | tf_op jit(solution)/shard_map/ppermute | solution.py:189
  16.3 0.8 %collective-permute-start.7 = (bf16[2,2,64,256]{3,2,1,0:T(8,128)(2,1)S(1)}, bf16[2,2,64,256]{3,2,1,0:T(8,128)(2,1)S(1)}, u32[]{:S(2)}, u32[]{:S(2)}) collective-permute-start(bf16[2,2,64,256]{3,2,1,0:T(8,128)(2,1)S(1)} %pad_maximum_fusion.1.refs_0_), channel_id=1, source_target_pairs={{0,8},{4,12},{8,0},{12,4},{16,24},{20,28},{24,16},{28,20},{1,9},{5... | collective-permute-start | bytes 393224 | tf_op jit(solution)/shard_map/ppermute | solution.py:189
  17.1 2.1 %collective-permute-start.8 = (bf16[2,2,64,256]{3,2,1,0:T(8,128)(2,1)S(1)}, bf16[2,2,64,256]{3,2,1,0:T(8,128)(2,1)S(1)}, u32[]{:S(2)}, u32[]{:S(2)}) collective-permute-start(bf16[2,2,64,256]{3,2,1,0:T(8,128)(2,1)S(1)} %pad_maximum_fusion.1.refs_0_), channel_id=1, source_target_pairs={{0,12},{4,8},{8,4},{12,0},{16,28},{20,24},{24,20},{28,16},{1,13},{... | collective-permute-start | bytes 393224 | tf_op jit(solution)/shard_map/ppermute | solution.py:189
  19.3 4.2 %shard_map.68 = (bf16[4,256,256]{2,1,0:T(8,128)(2,1)S(1)}, bf16[4,2,2,64,256]{4,3,2,1,0:T(8,128)(2,1)S(1)}, bf16[256,2048]{1,0:T(8,128)(2,1)S(1)}, bf16[2,256,256]{2,1,0:T(8,128)(2,1)S(1)}) custom-call(s32[2]{0:T(128)S(1)} %pad_add_fusion.place_ref, bf16[8,64,256]{2,1,0:T(8,128)(2,1)S(1)} %fusion.2.refs_0_, ...), custom_call_target="tpu_custom_call" | custom-call | flops 1073741824 | bytes 5242880 | tf_op jit(solution)/shard_map/pallas_call | solution.py:242
  23.5 0.6 %collective-permute-start.5 = (bf16[2,2,2,64,256]{4,3,2,1,0:T(8,128)(2,1)S(1)}, bf16[2,2,2,64,256]{4,3,2,1,0:T(8,128)(2,1)S(1)}, u32[]{:S(2)}, u32[]{:S(2)}) collective-permute-start(bf16[2,2,2,64,256]{4,3,2,1,0:T(8,128)(2,1)S(1)} %slice.69), channel_id=1, source_target_pairs={{0,4},{4,0},{8,12},{12,8},{16,20},{20,16},{24,28},{28,24},{1,5},{5... | collective-permute-start | bytes 786440 | tf_op jit(solution)/shard_map/ppermute | solution.py:189
  24.1 1.1 %collective-permute-done.8.refs_3_ = bf16[2,2,64,256]{3,2,1,0:T(8,128)(2,1)S(1)} collective-permute-done((bf16[2,2,64,256]{3,2,1,0:T(8,128)(2,1)S(1)}, bf16[2,2,64,256]{3,2,1,0:T(8,128)(2,1)S(1)}, u32[]{:S(2)}, u32[]{:S(2)}) %collective-permute-start.8) | collective-permute-done | bytes 131104 | tf_op jit(solution)/shard_map/ppermute | solution.py:189
  25.2 1.7 %shard_map.69 = (bf16[256,1024]{1,0:T(8,128)(2,1)S(1)}, bf16[1024,256]{1,0:T(8,128)(2,1)S(1)}, bf16[4,64,256]{2,1,0:T(8,128)(2,1)S(1)}) custom-call(s32[2]{0:T(128)S(1)} %pad_add_fusion.place_ref, bf16[2,2,64,256]{3,2,1,0:T(8,128)(2,1)S(1)} %pad_maximum_fusion.1.refs_0_, bf16[2,2,64,256]{3,2,1,0:T(8,128)(2,1)S(1)} %collective-permute-done.6.refs_1_, ...), custom_call_target="tpu_custom_call" | custom-call | flops 256 | bytes 256 | tf_op jit(solution)/shard_map/pallas_call | solution.py:268
  26.9 1.4 %collective-permute-start.10 = (bf16[64,256]{1,0:T(8,128)(2,1)S(1)}, bf16[64,256]{1,0:T(8,128)(2,1)S(1)}, u32[]{:S(2)}, u32[]{:S(2)}) collective-permute-start(bf16[64,256]{1,0:T(8,128)(2,1)S(1)} %get-tuple-element.80), channel_id=1, source_target_pairs={{0,2},{1,3},{2,0},{3,1},{4,6},{5,7},{6,4},{7,5},{8,10},{9,11},{10,... | collective-permute-start | bytes 98312 | tf_op jit(solution)/shard_map/ppermute | solution.py:192
  28.3 0.8 %collective-permute-start.9 = (bf16[64,256]{1,0:T(8,128)(2,1)S(1)}, bf16[64,256]{1,0:T(8,128)(2,1)S(1)}, u32[]{:S(2)}, u32[]{:S(2)}) collective-permute-start(bf16[64,256]{1,0:T(8,128)(2,1)S(1)} %get-tuple-element.78), channel_id=1, source_target_pairs={{0,1},{1,0},{2,3},{3,2},{4,5},{5,4},{6,7},{7,6},{8,9},{9,8},{10,11... | collective-permute-start | bytes 98312 | tf_op jit(solution)/shard_map/ppermute | solution.py:192
  29.1 1.6 %shard_map.70 = bf16[4,4,64,256]{3,2,1,0:T(8,128)(2,1)S(1)} custom-call(s32[2]{0:T(128)S(1)} %pad_add_fusion.place_ref, bf16[1024,256]{1,0:T(8,128)(2,1)S(1)} %get-tuple-element.55.wt_ref, bf16[2048,1024]{1,0:T(8,128)(2,1)S(1)} %copy-done), custom_call_target="tpu_custom_call" | custom-call | flops 256 | bytes 256 | tf_op jit(solution)/shard_map/pallas_call | solution.py:283
  30.9 0.8 %collective-permute-done.11 = bf16[64,256]{1,0:T(8,128)(2,1)S(1)} collective-permute-done((bf16[64,256]{1,0:T(8,128)(2,1)S(1)}, bf16[64,256]{1,0:T(8,128)(2,1)S(1)}, u32[]{:S(2)}, u32[]{:S(2)}) %collective-permute-start.11) | collective-permute-done | bytes 32800 | tf_op jit(solution)/shard_map/ppermute | solution.py:192
  31.9 1.2 %collective-permute-start.12 = (bf16[64,256]{1,0:T(8,128)(2,1)S(1)}, bf16[64,256]{1,0:T(8,128)(2,1)S(1)}, u32[]{:S(2)}, u32[]{:S(2)}) collective-permute-start(bf16[64,256]{1,0:T(8,128)(2,1)S(1)} %fusion.4), channel_id=1, source_target_pairs={{0,4},{4,0},{8,12},{12,8},{16,20},{20,16},{24,28},{28,24},{1,5},{5... | collective-permute-start | bytes 98312 | tf_op jit(solution)/shard_map/ppermute | solution.py:189
  33.1 1.6 %shard_map.71 = bf16[4,4,64,256]{3,2,1,0:T(8,128)(2,1)S(1)} custom-call(s32[2]{0:T(128)S(1)} %pad_add_fusion.place_ref, bf16[1024,256]{1,0:T(8,128)(2,1)S(1)} %get-tuple-element.55.wt_ref, bf16[2048,1024]{1,0:T(8,128)(2,1)S(1)} %copy-done), custom_call_target="tpu_custom_call" | custom-call | flops 256 | bytes 256 | tf_op jit(solution)/shard_map/pallas_call | solution.py:283
  34.7 1.2 %collective-permute-done.12 = bf16[64,256]{1,0:T(8,128)(2,1)S(1)} collective-permute-done((bf16[64,256]{1,0:T(8,128)(2,1)S(1)}, bf16[64,256]{1,0:T(8,128)(2,1)S(1)}, u32[]{:S(2)}, u32[]{:S(2)}) %collective-permute-start.12) | collective-permute-done | bytes 32800 | tf_op jit(solution)/shard_map/ppermute | solution.py:189
  36.0 1.8 %collective-permute-start.16 = (bf16[64,256]{1,0:T(8,128)(2,1)S(1)}, bf16[64,256]{1,0:T(8,128)(2,1)S(1)}, u32[]{:S(2)}, u32[]{:S(2)}) collective-permute-start(bf16[64,256]{1,0:T(8,128)(2,1)S(1)} %add_convert_fusion.4), channel_id=1, source_target_pairs={{0,8},{4,12},{8,0},{12,4},{16,24},{20,28},{24,16},{28,20},{1,9},{5... | collective-permute-start | bytes 98312 | tf_op jit(solution)/shard_map/ppermute | solution.py:189
  38.2 1.2 %collective-permute-start.14 = (bf16[1,4,64,256]{3,2,1,0:T(8,128)(2,1)S(1)}, bf16[1,4,64,256]{3,2,1,0:T(8,128)(2,1)S(1)}, u32[]{:S(2)}, u32[]{:S(2)}) collective-permute-start(bf16[1,4,64,256]{3,2,1,0:T(8,128)(2,1)S(1)} %slice.77), channel_id=1, source_target_pairs={{0,2},{1,3},{2,0},{3,1},{4,6},{5,7},{6,4},{7,5},{8,10},{9,11},{10,... | collective-permute-start | bytes 393224 | tf_op jit(solution)/shard_map/ppermute | solution.py:192
  39.4 3.4 %shard_map.72.refs_0_ = bf16[16384,128]{1,0:T(8,128)(2,1)} custom-call(bf16[256,2048]{1,0:T(8,128)(2,1)S(1)} %get-tuple-element.61.pt_ref, bf16[256,1024]{1,0:T(8,128)(2,1)S(1)} %get-tuple-element.66.w_ref, bf16[16384,128]{1,0:T(8,128)(2,1)S(1)} %bitcast.51), custom_call_target="tpu_custom_call" | custom-call | flops 805306368 | bytes 6291456 | tf_op jit(solution)/shard_map/pallas_call | solution.py:298
  42.8 0.7 %collective-permute-done.15 = bf16[1,2,2,64,256]{4,3,2,1,0:T(8,128)(2,1)S(1)} collective-permute-done((bf16[1,2,2,64,256]{4,3,2,1,0:T(8,128)(2,1)S(1)}, bf16[1,2,2,64,256]{4,3,2,1,0:T(8,128)(2,1)S(1)}, u32[]{:S(2)}, u32[]{:S(2)}) %collective-permute-start.15) | collective-permute-done | bytes 131104 | tf_op jit(solution)/shard_map/ppermute | solution.py:189
  43.7 2.7 %collective-permute-start.21 = (bf16[64,256]{1,0:T(8,128)(2,1)S(1)}, bf16[64,256]{1,0:T(8,128)(2,1)S(1)}, u32[]{:S(2)}, u32[]{:S(2)}) collective-permute-start(bf16[64,256]{1,0:T(8,128)(2,1)S(1)} %convert_add_fusion.5), channel_id=1, source_target_pairs={{0,16},{4,20},{8,24},{12,28},{16,0},{20,4},{24,8},{28,12},{1,17},{... | collective-permute-start | bytes 98312 | tf_op jit(solution)/shard_map/ppermute | solution.py:189
  46.4 1.2 %collective-permute-start.19 = (bf16[2,64,256]{2,1,0:T(8,128)(2,1)S(1)}, bf16[2,64,256]{2,1,0:T(8,128)(2,1)S(1)}, u32[]{:S(2)}, u32[]{:S(2)}) collective-permute-start(bf16[2,64,256]{2,1,0:T(8,128)(2,1)S(1)} %get-tuple-element.76), channel_id=1, source_target_pairs={{8,0},{12,1},{0,2},{4,3},{9,4},{13,5},{1,6},{5,7},{10,8},{14,9},{2... | collective-permute-start | bytes 196616 | tf_op jit(solution)/shard_map/ppermute | solution.py:204
  47.5 1.1 %collective-permute-start.20 = (bf16[2,64,256]{2,1,0:T(8,128)(2,1)S(1)}, bf16[2,64,256]{2,1,0:T(8,128)(2,1)S(1)}, u32[]{:S(2)}, u32[]{:S(2)}) collective-permute-start(bf16[2,64,256]{2,1,0:T(8,128)(2,1)S(1)} %get-tuple-element.77), channel_id=1, source_target_pairs={{24,0},{28,1},{16,2},{20,3},{25,4},{29,5},{17,6},{21,7},{26,8},{30... | collective-permute-start | bytes 196616 | tf_op jit(solution)/shard_map/ppermute | solution.py:204
  48.7 1.4 %collective-permute-start.18 = (bf16[1,4,64,256]{3,2,1,0:T(8,128)(2,1)S(1)}, bf16[1,4,64,256]{3,2,1,0:T(8,128)(2,1)S(1)}, u32[]{:S(2)}, u32[]{:S(2)}) collective-permute-start(bf16[1,4,64,256]{3,2,1,0:T(8,128)(2,1)S(1)} %slice.83), channel_id=1, source_target_pairs={{0,2},{1,3},{2,0},{3,1},{4,6},{5,7},{6,4},{7,5},{8,10},{9,11},{10,... | collective-permute-start | bytes 393224 | tf_op jit(solution)/shard_map/ppermute | solution.py:192
  50.0 1.7 %shard_map.73 = bf16[16384,128]{1,0:T(8,128)(2,1)} custom-call(bf16[256,2048]{1,0:T(8,128)(2,1)S(1)} %get-tuple-element.61.pt_ref, bf16[256,1024]{1,0:T(8,128)(2,1)S(1)} %get-tuple-element.66.w_ref, bf16[16384,128]{1,0:T(8,128)(2,1)S(1)} %bitcast.52, bf16[16384,128]{1,0:T(8,128)(2,1)} %shard_map.72.refs_0_), custom_call_target="tpu_custom_call", output_to_operand_aliasing={{}: (3, {})} | custom-call | flops 268435456 | bytes 2097152 | tf_op jit(solution)/shard_map/pallas_call | solution.py:298
  51.7 0.6 %convert_add_fusion.4 = f32[64,256]{1,0:T(8,128)} fusion(bf16[64,256]{1,0:T(8,128)(2,1)S(1)} %collective-permute-done.21, bf16[64,256]{1,0:T(8,128)(2,1)S(1)} %convert_add_fusion.5), kind=kLoop, calls=%fused_computation.18 | loop fusion | flops 49152 | bytes 131072 | tf_op jit(solution)/shard_map/add | solution.py:322
  52.4 1.3 %collective-permute-done.20 = bf16[2,64,256]{2,1,0:T(8,128)(2,1)S(1)} collective-permute-done((bf16[2,64,256]{2,1,0:T(8,128)(2,1)S(1)}, bf16[2,64,256]{2,1,0:T(8,128)(2,1)S(1)}, u32[]{:S(2)}, u32[]{:S(2)}) %collective-permute-start.20) | collective-permute-done | bytes 65568 | tf_op jit(solution)/shard_map/ppermute | solution.py:204
  53.9 0.8 %fusion.1 = f32[8,1,256,64]{2,3,1,0:T(8,128)} fusion(f32[4,64,256]{2,1,0:T(8,128)S(1)} %bitcast.56, f32[4,64,256]{2,1,0:T(8,128)S(1)} %bitcast.55, f32[2,64,256]{2,1,0:T(8,128)S(1)} %bitcast_add_fusion), kind=kLoop, calls=%fused_computation.2 | loop fusion | flops 524288 | bytes 1179648
  (52 shorter events, 2.5 us)
Async XLA Ops:
  0.6 18.7 %copy-start.2 = (f32[256,256]{1,0:T(8,128)S(1)}, f32[256,256]{1,0:T(8,128)}, u32[]{:S(2)}) copy-start(f32[256,256]{1,0:T(8,128)} %refs_5_.1) | copy-start | bytes 786436
  1.8 12.7 %collective-permute-start.2 = (bf16[8,64,256]{2,1,0:T(8,128)(2,1)S(1)}, bf16[8,64,256]{2,1,0:T(8,128)(2,1)S(1)}, u32[]{:S(2)}, u32[]{:S(2)}) collective-permute-start(bf16[8,64,256]{2,1,0:T(8,128)(2,1)S(1)} %fusion.2.refs_0_), channel_id=1, source_target_pairs={{0,1},{1,0},{2,3},{3,2},{4,5},{5,4},{6,7},{7,6},{8,9},{9,8},{10,11... | collective-permute-start | bytes 786440 | tf_op jit(solution)/shard_map/ppermute | solution.py:192
  2.3 12.2 %collective-permute-start.3 = (bf16[8,64,256]{2,1,0:T(8,128)(2,1)S(1)}, bf16[8,64,256]{2,1,0:T(8,128)(2,1)S(1)}, u32[]{:S(2)}, u32[]{:S(2)}) collective-permute-start(bf16[8,64,256]{2,1,0:T(8,128)(2,1)S(1)} %fusion.2.refs_0_), channel_id=1, source_target_pairs={{0,2},{1,3},{2,0},{3,1},{4,6},{5,7},{6,4},{7,5},{8,10},{9,11},{10,... | collective-permute-start | bytes 786440 | tf_op jit(solution)/shard_map/ppermute | solution.py:192
  4.8 9.1 %collective-permute-start = (bf16[2,64,256]{2,1,0:T(8,128)(2,1)S(1)}, bf16[2,64,256]{2,1,0:T(8,128)(2,1)S(1)}, u32[]{:S(2)}, u32[]{:S(2)}) collective-permute-start(bf16[2,64,256]{2,1,0:T(8,128)(2,1)S(1)} %slice.89), channel_id=1, source_target_pairs={{0,8},{1,12},{2,0},{3,4},{4,9},{5,13},{6,1},{7,5},{8,10},{9,14},{1... | collective-permute-start | bytes 196616 | tf_op jit(solution)/shard_map/ppermute | solution.py:204
  6.4 8.1 %collective-permute-start.1 = (bf16[2,64,256]{2,1,0:T(8,128)(2,1)S(1)}, bf16[2,64,256]{2,1,0:T(8,128)(2,1)S(1)}, u32[]{:S(2)}, u32[]{:S(2)}) collective-permute-start(bf16[2,64,256]{2,1,0:T(8,128)(2,1)S(1)} %slice.89), channel_id=1, source_target_pairs={{0,24},{1,28},{2,16},{3,20},{4,25},{5,29},{6,17},{7,21},{8,26},{9,... | collective-permute-start | bytes 196616 | tf_op jit(solution)/shard_map/ppermute | solution.py:204
  13.9 11.3 %copy-start.3 = (f32[8,128]{1,0:T(8,128)S(1)}, f32[8,128]{1,0:T(8,128)}, u32[]{:S(2)}) copy-start(f32[8,128]{1,0:T(8,128)} %get-tuple-element.48.refs_7_) | copy-start | bytes 12292
  14.5 4.8 %collective-permute-start.4 = (bf16[8,64,256]{2,1,0:T(8,128)(2,1)S(1)}, bf16[8,64,256]{2,1,0:T(8,128)(2,1)S(1)}, u32[]{:S(2)}, u32[]{:S(2)}) collective-permute-start(bf16[8,64,256]{2,1,0:T(8,128)(2,1)S(1)} %collective-permute-done.3.refs_2_), channel_id=1, source_target_pairs={{0,1},{1,0},{2,3},{3,2},{4,5},{5,4},{6,7},{7,6},{8,9},{9,8},{10,11... | collective-permute-start | bytes 786440 | tf_op jit(solution)/shard_map/ppermute | solution.py:192
  15.7 13.4 %copy-start = (bf16[2048,1024]{1,0:T(8,128)(2,1)S(1)}, bf16[2048,1024]{1,0:T(8,128)(2,1)}, u32[]{:S(2)}) copy-start(bf16[2048,1024]{1,0:T(8,128)(2,1)} %get-tuple-element.42.refs_5_.g_ref) | copy-start | bytes 12582916
  15.7 8.4 %collective-permute-start.6 = (bf16[2,2,64,256]{3,2,1,0:T(8,128)(2,1)S(1)}, bf16[2,2,64,256]{3,2,1,0:T(8,128)(2,1)S(1)}, u32[]{:S(2)}, u32[]{:S(2)}) collective-permute-start(bf16[2,2,64,256]{3,2,1,0:T(8,128)(2,1)S(1)} %pad_maximum_fusion.1.refs_0_), channel_id=1, source_target_pairs={{0,4},{4,0},{8,12},{12,8},{16,20},{20,16},{24,28},{28,24},{1,5},{5... | collective-permute-start | bytes 393224 | tf_op jit(solution)/shard_map/ppermute | solution.py:189
  16.3 7.8 %collective-permute-start.7 = (bf16[2,2,64,256]{3,2,1,0:T(8,128)(2,1)S(1)}, bf16[2,2,64,256]{3,2,1,0:T(8,128)(2,1)S(1)}, u32[]{:S(2)}, u32[]{:S(2)}) collective-permute-start(bf16[2,2,64,256]{3,2,1,0:T(8,128)(2,1)S(1)} %pad_maximum_fusion.1.refs_0_), channel_id=1, source_target_pairs={{0,8},{4,12},{8,0},{12,4},{16,24},{20,28},{24,16},{28,20},{1,9},{5... | collective-permute-start | bytes 393224 | tf_op jit(solution)/shard_map/ppermute | solution.py:189
  17.1 8.1 %collective-permute-start.8 = (bf16[2,2,64,256]{3,2,1,0:T(8,128)(2,1)S(1)}, bf16[2,2,64,256]{3,2,1,0:T(8,128)(2,1)S(1)}, u32[]{:S(2)}, u32[]{:S(2)}) collective-permute-start(bf16[2,2,64,256]{3,2,1,0:T(8,128)(2,1)S(1)} %pad_maximum_fusion.1.refs_0_), channel_id=1, source_target_pairs={{0,12},{4,8},{8,4},{12,0},{16,28},{20,24},{24,20},{28,16},{1,13},{... | collective-permute-start | bytes 393224 | tf_op jit(solution)/shard_map/ppermute | solution.py:189
  23.5 8.2 %collective-permute-start.5 = (bf16[2,2,2,64,256]{4,3,2,1,0:T(8,128)(2,1)S(1)}, bf16[2,2,2,64,256]{4,3,2,1,0:T(8,128)(2,1)S(1)}, u32[]{:S(2)}, u32[]{:S(2)}) collective-permute-start(bf16[2,2,2,64,256]{4,3,2,1,0:T(8,128)(2,1)S(1)} %slice.69), channel_id=1, source_target_pairs={{0,4},{4,0},{8,12},{12,8},{16,20},{20,16},{24,28},{28,24},{1,5},{5... | collective-permute-start | bytes 786440 | tf_op jit(solution)/shard_map/ppermute | solution.py:189
  26.9 4.0 %collective-permute-start.10 = (bf16[64,256]{1,0:T(8,128)(2,1)S(1)}, bf16[64,256]{1,0:T(8,128)(2,1)S(1)}, u32[]{:S(2)}, u32[]{:S(2)}) collective-permute-start(bf16[64,256]{1,0:T(8,128)(2,1)S(1)} %get-tuple-element.80), channel_id=1, source_target_pairs={{0,2},{1,3},{2,0},{3,1},{4,6},{5,7},{6,4},{7,5},{8,10},{9,11},{10,... | collective-permute-start | bytes 98312 | tf_op jit(solution)/shard_map/ppermute | solution.py:192
  28.3 3.3 %collective-permute-start.11 = (bf16[64,256]{1,0:T(8,128)(2,1)S(1)}, bf16[64,256]{1,0:T(8,128)(2,1)S(1)}, u32[]{:S(2)}, u32[]{:S(2)}) collective-permute-start(bf16[64,256]{1,0:T(8,128)(2,1)S(1)} %get-tuple-element.79), channel_id=1, source_target_pairs={{0,3},{1,2},{2,1},{3,0},{4,7},{5,6},{6,5},{7,4},{8,11},{9,10},{10,... | collective-permute-start | bytes 98312 | tf_op jit(solution)/shard_map/ppermute | solution.py:192
  28.3 3.3 %collective-permute-start.9 = (bf16[64,256]{1,0:T(8,128)(2,1)S(1)}, bf16[64,256]{1,0:T(8,128)(2,1)S(1)}, u32[]{:S(2)}, u32[]{:S(2)}) collective-permute-start(bf16[64,256]{1,0:T(8,128)(2,1)S(1)} %get-tuple-element.78), channel_id=1, source_target_pairs={{0,1},{1,0},{2,3},{3,2},{4,5},{5,4},{6,7},{7,6},{8,9},{9,8},{10,11... | collective-permute-start | bytes 98312 | tf_op jit(solution)/shard_map/ppermute | solution.py:192
  31.7 7.8 %copy-start.1 = (bf16[8,1,256,4,1,256]{5,3,4,2,1,0:T(4,128)(2,1)S(1)}, bf16[8,1,256,4,1,256]{5,3,4,2,1,0:T(4,128)(2,1)}, u32[]{:S(2)}) copy-start(bf16[8,1,256,4,1,256]{5,3,4,2,1,0:T(4,128)(2,1)} %param.5) | copy-start | bytes 12582916
  31.8 4.1 %collective-permute-start.13 = (bf16[2,4,64,256]{3,2,1,0:T(8,128)(2,1)S(1)}, bf16[2,4,64,256]{3,2,1,0:T(8,128)(2,1)S(1)}, u32[]{:S(2)}, u32[]{:S(2)}) collective-permute-start(bf16[2,4,64,256]{3,2,1,0:T(8,128)(2,1)S(1)} %slice.75), channel_id=1, source_target_pairs={{0,1},{1,0},{2,3},{3,2},{4,5},{5,4},{6,7},{7,6},{8,9},{9,8},{10,11... | collective-permute-start | bytes 786440 | tf_op jit(solution)/shard_map/ppermute | solution.py:192
  31.9 4.0 %collective-permute-start.12 = (bf16[64,256]{1,0:T(8,128)(2,1)S(1)}, bf16[64,256]{1,0:T(8,128)(2,1)S(1)}, u32[]{:S(2)}, u32[]{:S(2)}) collective-permute-start(bf16[64,256]{1,0:T(8,128)(2,1)S(1)} %fusion.4), channel_id=1, source_target_pairs={{0,4},{4,0},{8,12},{12,8},{16,20},{20,16},{24,28},{28,24},{1,5},{5... | collective-permute-start | bytes 98312 | tf_op jit(solution)/shard_map/ppermute | solution.py:189
  36.0 7.7 %collective-permute-start.17 = (bf16[2,4,64,256]{3,2,1,0:T(8,128)(2,1)S(1)}, bf16[2,4,64,256]{3,2,1,0:T(8,128)(2,1)S(1)}, u32[]{:S(2)}, u32[]{:S(2)}) collective-permute-start(bf16[2,4,64,256]{3,2,1,0:T(8,128)(2,1)S(1)} %slice.81), channel_id=1, source_target_pairs={{0,1},{1,0},{2,3},{3,2},{4,5},{5,4},{6,7},{7,6},{8,9},{9,8},{10,11... | collective-permute-start | bytes 786440 | tf_op jit(solution)/shard_map/ppermute | solution.py:192
  36.0 6.7 %collective-permute-start.16 = (bf16[64,256]{1,0:T(8,128)(2,1)S(1)}, bf16[64,256]{1,0:T(8,128)(2,1)S(1)}, u32[]{:S(2)}, u32[]{:S(2)}) collective-permute-start(bf16[64,256]{1,0:T(8,128)(2,1)S(1)} %add_convert_fusion.4), channel_id=1, source_target_pairs={{0,8},{4,12},{8,0},{12,4},{16,24},{20,28},{24,16},{28,20},{1,9},{5... | collective-permute-start | bytes 98312 | tf_op jit(solution)/shard_map/ppermute | solution.py:189
  37.9 5.6 %collective-permute-start.15 = (bf16[1,2,2,64,256]{4,3,2,1,0:T(8,128)(2,1)S(1)}, bf16[1,2,2,64,256]{4,3,2,1,0:T(8,128)(2,1)S(1)}, u32[]{:S(2)}, u32[]{:S(2)}) collective-permute-start(bf16[1,2,2,64,256]{4,3,2,1,0:T(8,128)(2,1)S(1)} %slice.79), channel_id=1, source_target_pairs={{0,8},{4,12},{8,0},{12,4},{16,24},{20,28},{24,16},{28,20},{1,9},{5... | collective-permute-start | bytes 393224 | tf_op jit(solution)/shard_map/ppermute | solution.py:189
  38.2 5.4 %collective-permute-start.14 = (bf16[1,4,64,256]{3,2,1,0:T(8,128)(2,1)S(1)}, bf16[1,4,64,256]{3,2,1,0:T(8,128)(2,1)S(1)}, u32[]{:S(2)}, u32[]{:S(2)}) collective-permute-start(bf16[1,4,64,256]{3,2,1,0:T(8,128)(2,1)S(1)} %slice.77), channel_id=1, source_target_pairs={{0,2},{1,3},{2,0},{3,1},{4,6},{5,7},{6,4},{7,5},{8,10},{9,11},{10,... | collective-permute-start | bytes 393224 | tf_op jit(solution)/shard_map/ppermute | solution.py:192
  43.7 8.0 %collective-permute-start.21 = (bf16[64,256]{1,0:T(8,128)(2,1)S(1)}, bf16[64,256]{1,0:T(8,128)(2,1)S(1)}, u32[]{:S(2)}, u32[]{:S(2)}) collective-permute-start(bf16[64,256]{1,0:T(8,128)(2,1)S(1)} %convert_add_fusion.5), channel_id=1, source_target_pairs={{0,16},{4,20},{8,24},{12,28},{16,0},{20,4},{24,8},{28,12},{1,17},{... | collective-permute-start | bytes 98312 | tf_op jit(solution)/shard_map/ppermute | solution.py:189
  46.4 6.0 %collective-permute-start.19 = (bf16[2,64,256]{2,1,0:T(8,128)(2,1)S(1)}, bf16[2,64,256]{2,1,0:T(8,128)(2,1)S(1)}, u32[]{:S(2)}, u32[]{:S(2)}) collective-permute-start(bf16[2,64,256]{2,1,0:T(8,128)(2,1)S(1)} %get-tuple-element.76), channel_id=1, source_target_pairs={{8,0},{12,1},{0,2},{4,3},{9,4},{13,5},{1,6},{5,7},{10,8},{14,9},{2... | collective-permute-start | bytes 196616 | tf_op jit(solution)/shard_map/ppermute | solution.py:204
  47.5 6.2 %collective-permute-start.20 = (bf16[2,64,256]{2,1,0:T(8,128)(2,1)S(1)}, bf16[2,64,256]{2,1,0:T(8,128)(2,1)S(1)}, u32[]{:S(2)}, u32[]{:S(2)}) collective-permute-start(bf16[2,64,256]{2,1,0:T(8,128)(2,1)S(1)} %get-tuple-element.77), channel_id=1, source_target_pairs={{24,0},{28,1},{16,2},{20,3},{25,4},{29,5},{17,6},{21,7},{26,8},{30... | collective-permute-start | bytes 196616 | tf_op jit(solution)/shard_map/ppermute | solution.py:204
  48.7 5.2 %collective-permute-start.18 = (bf16[1,4,64,256]{3,2,1,0:T(8,128)(2,1)S(1)}, bf16[1,4,64,256]{3,2,1,0:T(8,128)(2,1)S(1)}, u32[]{:S(2)}, u32[]{:S(2)}) collective-permute-start(bf16[1,4,64,256]{3,2,1,0:T(8,128)(2,1)S(1)} %slice.83), channel_id=1, source_target_pairs={{0,2},{1,3},{2,0},{3,1},{4,6},{5,7},{6,4},{7,5},{8,10},{9,11},{10,... | collective-permute-start | bytes 393224 | tf_op jit(solution)/shard_map/ppermute | solution.py:192
